TPU v7x, 256 devices: a whole 4x4x8 slice. The times are simulated.
256 devices in a mesh: train: 32 (over y_hi, z, core), cand: 8 (over x, y_lo).
Axes of the slice: x: 4, y: 4 (y_hi: 2, y_lo: 2; y = y_hi * 2 + y_lo), z: 8, core: 2. Of those that a mesh axis runs over, the one named last changes fastest.
Arguments:
- x_train: float32 [8, 16384], P(None, 'train'), may hold values from -4 to 4
- x_cand: float32 [8, 8192], P(None, 'cand'), may hold values from -4 to 4
- targets: float32 [16384], P(('train', 'cand')), may hold values from -6 to 6
- noise: float32 [16384, 64], P(('train', 'cand')), may hold values from -5 to 5
- omega: float32 [8, 4096], replicated, may hold values from -6 to 6
- phase: float32 [4096], replicated, may hold values from -3.140625 to 3.140625
- prior_weights: bfloat16 [4096, 64], P('cand'), may hold values from -6 to 6
Outputs:
- samples: float32 [8192, 64], P(('cand', 'train'))
- solution: float32 [16384, 64], P(('train', 'cand'))
All inputs are finite; a program needn't handle non-finite values.
Results may differ from a plain program's by a relative error of at most 0.0019.
The roundings to bfloat16 on the way count: a program that leaves them out, or rounds other values in their place, can miss the bound.
Values may be sent and summed in bfloat16 or wider, within the bound.
A program may use at most 64 MiB of HBM per device.

v0:
```python
import math
import jax
import jax.numpy as jnp
from jax import lax
from jax.sharding import PartitionSpec as P

ITERS = 2
noise_level = 0.5


def squares_of(points):
    return jnp.sum(points * points, axis=0)


def kernel_tile(row_points, row_norms, column_points, column_norms):
    inner = jnp.dot(row_points.T, column_points, precision=lax.Precision.HIGHEST)
    return jnp.exp(-0.5 * (row_norms[:, None] + column_norms[None, :] - 2.0 * inner)).astype(
        jnp.bfloat16
    )


def features(points, omega, phase):
    angles = jnp.dot(points.T, omega, precision=lax.Precision.HIGHEST) + phase[None, :]
    return (math.sqrt(2.0 / omega.shape[1]) * jnp.cos(angles)).astype(jnp.bfloat16)


def kernel_rows(points, every_point, every_norm, weights):
    count = points.shape[1]
    size = math.gcd(count, 1024)
    stacked = points.reshape(points.shape[0], count // size, size).transpose(1, 0, 2)

    def one_block(block_points):
        tile = kernel_tile(block_points, squares_of(block_points), every_point, every_norm)
        return jnp.dot(tile, weights, preferred_element_type=jnp.float32)

    return lax.map(one_block, stacked).reshape(count, weights.shape[1])


def body(x_train, x_cand, targets, noise, omega, phase, prior_weights):
    own_rows = noise.shape[0]
    cand_index = lax.axis_index("cand")
    train_index = lax.axis_index("train")
    own_points = lax.dynamic_slice_in_dim(x_train, cand_index * own_rows, own_rows, 1)
    full_weights = lax.all_gather(prior_weights, "cand", axis=0, tiled=True)
    prior_train = jnp.dot(
        features(own_points, omega, phase), full_weights, preferred_element_type=jnp.float32
    )
    rhs = targets[:, None] - prior_train - noise
    column_points = lax.all_gather(x_train, "train", axis=1, tiled=True)
    row_norms = squares_of(own_points)
    column_norms = squares_of(column_points)
    width = max(128, 262144 // own_points.shape[1])

    def squares(values):
        return lax.psum(jnp.sum(values * values, axis=0), ("train", "cand"))

    solution = jnp.zeros(rhs.shape, jnp.float32)
    residual = rhs
    direction = rhs
    norm_now = squares(residual)
    for step in range(ITERS):
        packed = direction.astype(jnp.bfloat16)
        empty = jnp.zeros((own_points.shape[1], packed.shape[1]), jnp.float32)
        total = empty
        piece = lax.all_gather(packed, ("train", "cand"), axis=0, tiled=True)
        for offset in range(0, piece.shape[0], width):
            count = min(width, piece.shape[0] - offset)
            accumulate_points = lax.dynamic_slice_in_dim(column_points, offset, count, 1)
            norms = lax.dynamic_slice_in_dim(column_norms, offset, count, 0)
            tile = kernel_tile(own_points, row_norms, accumulate_points, norms)
            total = total + jnp.dot(
                tile, piece[offset : offset + count], preferred_element_type=jnp.float32
            )
        image = total + noise_level * direction
        curve = lax.psum(jnp.sum(direction * image, axis=0), ("train", "cand"))
        alpha = norm_now / curve
        solution = solution + alpha * direction
        residual = residual - alpha * image
        norm_next = squares(residual)
        direction = residual + norm_next / norm_now * direction
        norm_now = norm_next
    per_device = x_cand.shape[1] // lax.axis_size("train")
    mine = lax.dynamic_slice_in_dim(x_cand, train_index * per_device, per_device, 1)
    packed_solution = solution.astype(jnp.bfloat16)
    block_weights = lax.all_gather(packed_solution, "cand", axis=0, tiled=True)
    train_norms = squares_of(x_train)
    kernel_part = lax.psum_scatter(
        kernel_rows(x_cand, x_train, train_norms, block_weights),
        "train",
        scatter_dimension=0,
        tiled=True,
    )
    prior_cand = jnp.dot(
        features(mine, omega, phase), full_weights, preferred_element_type=jnp.float32
    )
    return (prior_cand + kernel_part, solution)


def solution(mesh):
    placed = (
        P(None, "train"),
        P(None, "cand"),
        P(("train", "cand")),
        P(("train", "cand"), None),
        P(),
        P(),
        P("cand", None),
    )
    return jax.shard_map(
        body,
        mesh=mesh,
        in_specs=placed,
        out_specs=(P(("cand", "train"), None), P(("train", "cand"), None)),
        check_vma=False,
    )
```

profile of v0, /device:TPU:4, one launch (start us, length us, event | category | flops | bytes accessed | tf_op | source)
XLA Modules:
  0.0 1849.0 jit_solution(14359610649674526647)
XLA Ops:
  7.2 27.6 %all_gather.15 = bf16[4096,64]{0,1:T(8,128)(2,1)S(1)} all-gather(bf16[512,64]{0,1:T(8,128)(2,1)} %param.13), channel_id=1, replica_groups=mesh['train'=32,'cand'=8] {'cand'}, dimensions={0}, use_global_device_ids=true | all-gather | bytes 589824 | tf_op jit(solution)/shard_map/all_gather | solution.py:44
  34.9 5.5 fusion.14
  40.3 1.7 fusion.56
  42.1 0.8 multiply_reduce_fusion.6
  42.9 44.9 %all_gather.16 = f32[8,16384]{1,0:T(8,128)S(1)} all-gather(f32[8,512]{1,0:T(8,128)} %param.7), channel_id=1, replica_groups=mesh['train'=32,'cand'=8] {'train'}, dimensions={1}, use_global_device_ids=true | all-gather | bytes 540672 | tf_op jit(solution)/shard_map/all_gather | solution.py:49
  87.8 0.2 multiply_reduce_fusion
  87.9 2.0 fusion.15
  89.9 1.2 fusion.16
  91.2 1.3 fusion.17
  92.4 1.2 fusion.18
  93.7 654.8 %all-gather.3.cloned.1.call-done = bf16[16384,64]{1,0:T(8,128)(2,1)} async-done(((bf16[64,64]{1,0:T(8,128)(2,1)}), bf16[16384,64]{1,0:T(8,128)(2,1)}) %all-gather.3.cloned.1.call-update) | async-done | bytes 2097168 | tf_op jit(solution)/shard_map/all_gather | solution.py:65
  748.5 1.5 fusion.35
  750.1 1.5 convolution_add_fusion.7
  751.6 1.5 convolution_add_fusion.6
  753.2 1.6 multiply_reduce_fusion.2
  754.7 82.4 %all-reduce = (f32[64]{0:T(128)S(1)}, f32[64]{0:T(128)S(1)}) all-reduce(f32[64]{0:T(128)S(1)} %get-tuple-element.15, f32[64]{0:T(128)S(1)} %get-tuple-element.14), channel_id=1, replica_groups=mesh['train'=32,'cand'=8] {'train','cand'}, use_global_device_ids=true, to_apply=%region_3.0 | all-reduce | flops 128 | bytes 1024 | tf_op jit(solution)/shard_map/psum | solution.py:55
  837.2 72.7 %psum.30 = f32[64]{0:T(128)S(1)} all-reduce(f32[64]{0:T(128)S(1)} %multiply_reduce_fusion.1), channel_id=1, replica_groups=mesh['train'=32,'cand'=8] {'train','cand'}, use_global_device_ids=true, to_apply=%region_9.0 | all-reduce | flops 64 | bytes 512 | tf_op jit(solution)/shard_map/psum | solution.py:55
  909.9 0.6 fusion.53
  910.5 0.2 reduce-scatter.2.cloned.1.call-start
  910.8 2.2 exponential_convert_fusion
  913.0 698.1 %all-gather.5.cloned.1.call-done = bf16[16384,64]{1,0:T(8,128)(2,1)} async-done(((bf16[64,64]{1,0:T(8,128)(2,1)}), bf16[16384,64]{1,0:T(8,128)(2,1)}) %all-gather.5.cloned.1.call-update) | async-done | bytes 2097168 | tf_op jit(solution)/shard_map/all_gather | solution.py:65
  1611.1 1.7 fusion.30
  1612.8 1.5 convolution_add_fusion.4
  1614.4 1.5 convolution_add_fusion.3
  1615.9 1.6 fusion.26
  1617.5 82.4 %psum.31 = f32[64]{0:T(128)S(1)} all-reduce(f32[64]{0:T(128)S(1)} %fusion.26), channel_id=1, replica_groups=mesh['train'=32,'cand'=8] {'train','cand'}, use_global_device_ids=true, to_apply=%region_11.12 | all-reduce | flops 64 | bytes 512 | tf_op jit(solution)/shard_map/psum | solution.py:75
  1699.9 0.6 fusion.54
  1700.5 26.1 %all_gather.19 = bf16[512,64]{1,0:T(8,128)(2,1)S(1)} all-gather(bf16[64,64]{1,0:T(8,128)(2,1)S(1)} %get-tuple-element.24), channel_id=1, replica_groups=mesh['train'=32,'cand'=8] {'cand'}, dimensions={0}, use_global_device_ids=true | all-gather | bytes 73728 | tf_op jit(solution)/shard_map/all_gather | solution.py:85
  1726.6 1.2 fusion.57
  1727.8 2.7 fusion.21
  1730.5 110.3 %reduce-scatter.2.cloned.1.call-done = f32[32,64]{1,0:T(8,128)} async-done(((f32[1024,64]{1,0:T(8,128)}), f32[32,64]{1,0:T(8,128)}) %reduce-scatter.2.cloned.1.call-update) | async-done | bytes 8208 | tf_op jit(solution)/shard_map/reduce_scatter | solution.py:87
  1840.8 1.6 convolution_add_fusion.8
  (22 shorter events, 0.2 us)
Async XLA Ops:
  7.2 27.7 %copy-start = (f32[8,4096]{1,0:T(8,128)S(1)}, f32[8,4096]{1,0:T(8,128)}, u32[]{:S(2)}) copy-start(f32[8,4096]{1,0:T(8,128)} %param.11) | copy-start | bytes 393220
  7.2 82.7 %copy-start.1 = (f32[8,512]{1,0:T(8,128)S(1)}, f32[8,512]{1,0:T(8,128)}, u32[]{:S(2)}) copy-start(f32[8,512]{1,0:T(8,128)} %param.7) | copy-start | bytes 49156
  7.2 741.3 %all-gather.3.cloned.1.call-start = ((), (), s32[]{:S(2)}) async-start(), calls=%async_computation.1 | async-start | bytes 4210688 | tf_op jit(solution)/shard_map/all_gather | solution.py:65
  42.1 1569.1 %all-gather.5.cloned.1.call-start = ((), (), s32[]{:S(2)}) async-start(), calls=%async_computation.2 | async-start | bytes 4210688 | tf_op jit(solution)/shard_map/all_gather | solution.py:65
  92.4 818.4 %copy-start.3 = (f32[8,1024]{1,0:T(8,128)S(1)}, f32[8,1024]{1,0:T(8,128)}, u32[]{:S(2)}) copy-start(f32[8,1024]{1,0:T(8,128)} %param.8) | copy-start | bytes 98308
  93.7 659.5 %copy-start.4 = (bf16[64,4096]{1,0:T(8,128)(2,1)}, bf16[64,4096]{1,0:T(8,128)(2,1)S(1)}, u32[]{:S(2)}) copy-start(bf16[64,4096]{1,0:T(8,128)(2,1)S(1)} %fusion.18) | copy-start | bytes 1572868
  910.5 930.3 %reduce-scatter.2.cloned.1.call-start = ((), (), s32[]{:S(2)}) async-start(), calls=%async_computation.3 | async-start | bytes 540672 | tf_op jit(solution)/shard_map/reduce_scatter | solution.py:87
  913.0 814.8 %copy-start.2 = (f32[4096]{0:T(1024)S(1)}, f32[4096]{0:T(1024)}, u32[]{:S(2)}) copy-start(f32[4096]{0:T(1024)} %param.12) | copy-start | bytes 49156
Sparse Core Ops, SparseCore 0:
  42.2 706.2 all-gather.2
  910.7 700.4 all-gather.4
  1727.9 112.8 reduce-scatter.1
where the time goes:
time: 1850 us
  waiting for transfers between devices  1460 us (79%)
  blocking collectives  336 us (18%)
  matrix products  33.1 us (2%)
    all_gather x2, waiting for transfers between devices, body(): piece = lax.all_gather(packed, ('train', 'cand'), axis=0, tiled=True)  1350 us
    psum x2, blocking collectives, squares(): return lax.psum(jnp.sum(values * values, axis=0), ('train', 'cand'))  155 us
    reduce_scatter x1, waiting for transfers between devices, body(): lax.psum_scatter(kernel_rows(x_cand, x_train, train_norms, block_weights)...  110 us
    psum x1, blocking collectives, body(): curve = lax.psum(jnp.sum(direction * image, axis=0), ('train', 'cand'))  82.4 us
    all_gather x1, blocking collectives, body(): column_points = lax.all_gather(x_train, 'train', axis=1, tiled=True)  44.9 us
  transfers between devices with their start and end apart: 3, of which 3 were waited for; matrix products, arithmetic and copies ran while one was open for 1% of the time, Pallas kernels for 0%

commit v1 on v0

--- a/solution.py
+++ b/solution.py
@@ -72,7 +72,7 @@
                 tile, piece[offset : offset + count], preferred_element_type=jnp.float32
             )
         image = total + noise_level * direction
-        curve = lax.psum(jnp.sum(direction * image, axis=0), ("train", "cand"))
+        curve = lax.psum(lax.psum(jnp.sum(direction * image, axis=0), "cand"), "train")
         alpha = norm_now / curve
         solution = solution + alpha * direction
         residual = residual - alpha * image

time: 1850 us -> 1930 us (1.043)
  blocking collectives: 336 us -> 416 us
    psum x1 -> x4, blocking collectives: 82.4 us -> 165 us  [the longest x2 130 us: body(): lax.psum(lax.psum(jnp.sum(direction * image, axis=0), 'cand'), 'train')]
where the time goes in v1:
time: 1930 us
  waiting for transfers between devices  1460 us (76%)
  blocking collectives  416 us (22%)
  matrix products  33.1 us (2%)
    all_gather x2, waiting for transfers between devices, body(): piece = lax.all_gather(packed, ('train', 'cand'), axis=0, tiled=True)  1350 us
    psum x2, blocking collectives, squares(): return lax.psum(jnp.sum(values * values, axis=0), ('train', 'cand'))  149 us
    psum x2, blocking collectives, body(): lax.psum(lax.psum(jnp.sum(direction * image, axis=0), 'cand'), 'train')  130 us
    reduce_scatter x1, waiting for transfers between devices, body(): lax.psum_scatter(kernel_rows(x_cand, x_train, train_norms, block_weights)...  109 us
    all_gather x1, blocking collectives, body(): column_points = lax.all_gather(x_train, 'train', axis=1, tiled=True)  44.9 us
  transfers between devices with their start and end apart: 3, of which 3 were waited for; matrix products, arithmetic and copies ran while one was open for 1% of the time, Pallas kernels for 0%

profile of v1, /device:TPU:4, one launch (start us, length us, event | category | flops | bytes accessed | tf_op | source)
XLA Modules:
  0.0 1925.2 jit_solution(1339160358012722873)
XLA Ops:
  7.2 27.6 %all_gather.15 = bf16[4096,64]{0,1:T(8,128)(2,1)S(1)} all-gather(bf16[512,64]{0,1:T(8,128)(2,1)} %param.13), channel_id=1, replica_groups=mesh['train'=32,'cand'=8] {'cand'}, dimensions={0}, use_global_device_ids=true | all-gather | bytes 589824 | tf_op jit(solution)/shard_map/all_gather | solution.py:44
  34.9 5.5 fusion.14
  40.3 1.7 fusion.56
  42.1 0.8 multiply_reduce_fusion.6
  42.9 44.9 %all_gather.16 = f32[8,16384]{1,0:T(8,128)S(1)} all-gather(f32[8,512]{1,0:T(8,128)} %param.7), channel_id=1, replica_groups=mesh['train'=32,'cand'=8] {'train'}, dimensions={1}, use_global_device_ids=true | all-gather | bytes 540672 | tf_op jit(solution)/shard_map/all_gather | solution.py:49
  87.9 2.0 fusion.15
  89.9 1.2 fusion.16
  91.2 1.3 fusion.17
  92.4 1.2 fusion.18
  93.7 654.8 %all-gather.3.cloned.1.call-done = bf16[16384,64]{1,0:T(8,128)(2,1)} async-done(((bf16[64,64]{1,0:T(8,128)(2,1)}), bf16[16384,64]{1,0:T(8,128)(2,1)}) %all-gather.3.cloned.1.call-update) | async-done | bytes 2097168 | tf_op jit(solution)/shard_map/all_gather | solution.py:65
  748.5 1.5 fusion.35
  750.1 1.5 convolution_add_fusion.7
  751.6 1.5 convolution_add_fusion.6
  753.2 1.6 multiply_reduce_fusion.2
  754.7 17.7 psum.43
  772.4 65.0 %psum.44 = f32[64]{0:T(128)S(1)} all-reduce(f32[64]{0:T(128)S(1)} %psum.43), channel_id=1, replica_groups=mesh['train'=32,'cand'=8] {'train'}, use_global_device_ids=true, to_apply=%region_8.0 | all-reduce | flops 64 | bytes 512 | tf_op jit(solution)/shard_map/psum | solution.py:75
  837.4 75.9 %psum.42 = f32[64]{0:T(128)S(1)} all-reduce(f32[64]{0:T(128)S(1)} %get-tuple-element.15), channel_id=1, replica_groups=mesh['train'=32,'cand'=8] {'train','cand'}, use_global_device_ids=true, to_apply=%region_3.0 | all-reduce | flops 64 | bytes 512 | tf_op jit(solution)/shard_map/psum | solution.py:55
  913.3 73.6 %psum.45 = f32[64]{0:T(128)S(1)} all-reduce(f32[64]{0:T(128)S(1)} %multiply_reduce_fusion.1), channel_id=1, replica_groups=mesh['train'=32,'cand'=8] {'train','cand'}, use_global_device_ids=true, to_apply=%region_10.0 | all-reduce | flops 64 | bytes 512 | tf_op jit(solution)/shard_map/psum | solution.py:55
  987.8 2.2 exponential_convert_fusion
  990.0 695.8 %all-gather.5.cloned.1.call-done = bf16[16384,64]{1,0:T(8,128)(2,1)} async-done(((bf16[64,64]{1,0:T(8,128)(2,1)}), bf16[16384,64]{1,0:T(8,128)(2,1)}) %all-gather.5.cloned.1.call-update) | async-done | bytes 2097168 | tf_op jit(solution)/shard_map/all_gather | solution.py:65
  1685.8 1.7 fusion.30
  1687.5 1.5 convolution_add_fusion.4
  1689.1 1.5 convolution_add_fusion.3
  1690.6 1.6 fusion.26
  1692.2 17.7 psum.46
  1709.8 65.0 %psum.47 = f32[64]{0:T(128)S(1)} all-reduce(f32[64]{0:T(128)S(1)} %psum.46), channel_id=1, replica_groups=mesh['train'=32,'cand'=8] {'train'}, use_global_device_ids=true, to_apply=%region_13.14 | all-reduce | flops 64 | bytes 512 | tf_op jit(solution)/shard_map/psum | solution.py:75
  1774.8 0.6 fusion.54
  1775.5 28.5 %all_gather.19 = bf16[512,64]{1,0:T(8,128)(2,1)S(1)} all-gather(bf16[64,64]{1,0:T(8,128)(2,1)S(1)} %get-tuple-element.16), channel_id=1, replica_groups=mesh['train'=32,'cand'=8] {'cand'}, dimensions={0}, use_global_device_ids=true | all-gather | bytes 73728 | tf_op jit(solution)/shard_map/all_gather | solution.py:85
  1803.9 1.2 fusion.57
  1805.2 2.7 fusion.21
  1807.9 109.2 %reduce-scatter.2.cloned.1.call-done = f32[32,64]{1,0:T(8,128)} async-done(((f32[1024,64]{1,0:T(8,128)}), f32[32,64]{1,0:T(8,128)}) %reduce-scatter.2.cloned.1.call-update) | async-done | bytes 8208 | tf_op jit(solution)/shard_map/reduce_scatter | solution.py:87
  1917.1 1.6 convolution_add_fusion.8
  (25 shorter events, 1.3 us)
Async XLA Ops:
  7.2 27.7 %copy-start = (f32[8,4096]{1,0:T(8,128)S(1)}, f32[8,4096]{1,0:T(8,128)}, u32[]{:S(2)}) copy-start(f32[8,4096]{1,0:T(8,128)} %param.11) | copy-start | bytes 393220
  7.2 82.7 %copy-start.1 = (f32[8,512]{1,0:T(8,128)S(1)}, f32[8,512]{1,0:T(8,128)}, u32[]{:S(2)}) copy-start(f32[8,512]{1,0:T(8,128)} %param.7) | copy-start | bytes 49156
  7.2 741.3 %all-gather.3.cloned.1.call-start = ((), (), s32[]{:S(2)}) async-start(), calls=%async_computation.1 | async-start | bytes 4210688 | tf_op jit(solution)/shard_map/all_gather | solution.py:65
  42.1 1643.8 %all-gather.5.cloned.1.call-start = ((), (), s32[]{:S(2)}) async-start(), calls=%async_computation.2 | async-start | bytes 4210688 | tf_op jit(solution)/shard_map/all_gather | solution.py:65
  92.4 895.4 %copy-start.3 = (f32[8,1024]{1,0:T(8,128)S(1)}, f32[8,1024]{1,0:T(8,128)}, u32[]{:S(2)}) copy-start(f32[8,1024]{1,0:T(8,128)} %param.8) | copy-start | bytes 98308
  93.7 659.5 %copy-start.4 = (bf16[64,4096]{1,0:T(8,128)(2,1)}, bf16[64,4096]{1,0:T(8,128)(2,1)S(1)}, u32[]{:S(2)}) copy-start(bf16[64,4096]{1,0:T(8,128)(2,1)S(1)} %fusion.18) | copy-start | bytes 1572868
  987.5 929.6 %reduce-scatter.2.cloned.1.call-start = ((), (), s32[]{:S(2)}) async-start(), calls=%async_computation.3 | async-start | bytes 540672 | tf_op jit(solution)/shard_map/reduce_scatter | solution.py:87
  990.0 815.2 %copy-start.2 = (f32[4096]{0:T(1024)S(1)}, f32[4096]{0:T(1024)}, u32[]{:S(2)}) copy-start(f32[4096]{0:T(1024)} %param.12) | copy-start | bytes 49156
Sparse Core Ops, SparseCore 0:
  42.2 706.2 all-gather.2
  987.6 698.1 all-gather.4
  1805.3 111.7 reduce-scatter.1

commit v2 on v0

--- a/solution.py
+++ b/solution.py
@@ -72,7 +72,9 @@
                 tile, piece[offset : offset + count], preferred_element_type=jnp.float32
             )
         image = total + noise_level * direction
-        curve = lax.psum(jnp.sum(direction * image, axis=0), ("train", "cand"))
+        curve = jnp.sum(
+            lax.all_gather(jnp.sum(direction * image, axis=0), ("train", "cand")), axis=0
+        )
         alpha = norm_now / curve
         solution = solution + alpha * direction
         residual = residual - alpha * image

time: 1850 us -> 2170 us (1.17)
  waiting for transfers between devices: 1460 us -> 1860 us
  blocking collectives: 336 us -> 255 us
    unnamed x3 -> x7, waiting for transfers between devices: 0.05 us -> 398 us
    psum x1 -> x0, blocking collectives: 82.4 us -> none  [body(): curve = lax.psum(jnp.sum(direction * image, axis=0), ('train', 'cand'))]
  transfers between devices with their start and end apart: 3 -> 5, of which waited for: 3 -> 5; matrix products, arithmetic and copies ran while one was open for 1% -> 1% of each run, Pallas kernels for 0% -> 0%
where the time goes in v2:
time: 2170 us
  waiting for transfers between devices  1860 us (86%)
  blocking collectives  255 us (12%)
  matrix products  32.9 us (2%)
    all_gather x2, waiting for transfers between devices, body(): piece = lax.all_gather(packed, ('train', 'cand'), axis=0, tiled=True)  1350 us
    unnamed x7, waiting for transfers between devices  398 us
    psum x2, blocking collectives, squares(): return lax.psum(jnp.sum(values * values, axis=0), ('train', 'cand'))  157 us
    reduce_scatter x1, waiting for transfers between devices, body(): lax.psum_scatter(kernel_rows(x_cand, x_train, train_norms, block_weights)...  111 us
    all_gather x1, blocking collectives, body(): column_points = lax.all_gather(x_train, 'train', axis=1, tiled=True)  44.9 us
  transfers between devices with their start and end apart: 5, of which 5 were waited for; matrix products, arithmetic and copies ran while one was open for 1% of the time, Pallas kernels for 0%

profile of v2, /device:TPU:4, one launch (start us, length us, event | category | flops | bytes accessed | tf_op | source)
XLA Modules:
  0.0 2170.0 jit_solution(6230876157154317989)
XLA Ops:
  7.2 27.6 %all_gather.27 = bf16[4096,64]{0,1:T(8,128)(2,1)S(1)} all-gather(bf16[512,64]{0,1:T(8,128)(2,1)} %param.13), channel_id=1, replica_groups=mesh['train'=32,'cand'=8] {'cand'}, dimensions={0}, use_global_device_ids=true | all-gather | bytes 589824 | tf_op jit(solution)/shard_map/all_gather | solution.py:44
  34.9 5.5 fusion.14
  40.3 1.7 fusion.56
  42.1 0.8 multiply_reduce_fusion.6
  42.9 44.9 %all_gather.28 = f32[8,16384]{1,0:T(8,128)S(1)} all-gather(f32[8,512]{1,0:T(8,128)} %param.7), channel_id=1, replica_groups=mesh['train'=32,'cand'=8] {'train'}, dimensions={1}, use_global_device_ids=true | all-gather | bytes 540672 | tf_op jit(solution)/shard_map/all_gather | solution.py:49
  88.0 1.9 fusion.15
  89.9 1.2 fusion.16
  91.2 1.3 fusion.17
  92.4 1.2 fusion.18
  93.7 654.8 %all-gather.5.cloned.1.call-done = bf16[16384,64]{1,0:T(8,128)(2,1)} async-done(((bf16[64,64]{1,0:T(8,128)(2,1)}), bf16[16384,64]{1,0:T(8,128)(2,1)}) %all-gather.5.cloned.1.call-update) | async-done | bytes 2097168 | tf_op jit(solution)/shard_map/all_gather | solution.py:65
  748.5 1.5 fusion.35
  750.1 1.5 convolution_add_fusion.7
  751.6 1.5 convolution_add_fusion.6
  753.2 1.6 multiply_reduce_fusion.2
  755.7 82.9 %psum.14 = f32[64]{0:T(128)S(1)} all-reduce(f32[64]{0:T(128)S(1)} %get-tuple-element.15), channel_id=1, replica_groups=mesh['train'=32,'cand'=8] {'train','cand'}, use_global_device_ids=true, to_apply=%region_3.0 | all-reduce | flops 64 | bytes 512 | tf_op jit(solution)/shard_map/psum | solution.py:55
  838.6 158.7 %all-reduce.5.cloned.1.call-done = f32[16384]{0:T(1024)} async-done(((f32[16384]{0:T(1024)}), f32[16384]{0:T(1024)}) %all-reduce.5.cloned.1.call-update) | async-done | bytes 65552
  997.3 0.9 reshape.20
  998.3 74.2 %psum.15 = f32[64]{0:T(128)S(1)} all-reduce(f32[64]{0:T(128)S(1)} %multiply_reduce_fusion.1), channel_id=1, replica_groups=mesh['train'=32,'cand'=8] {'train','cand'}, use_global_device_ids=true, to_apply=%region_9.0 | all-reduce | flops 64 | bytes 512 | tf_op jit(solution)/shard_map/psum | solution.py:55
  1073.3 697.9 %all-gather.7.cloned.1.call-done = bf16[16384,64]{1,0:T(8,128)(2,1)} async-done(((bf16[64,64]{1,0:T(8,128)(2,1)}), bf16[16384,64]{1,0:T(8,128)(2,1)}) %all-gather.7.cloned.1.call-update) | async-done | bytes 2097168 | tf_op jit(solution)/shard_map/all_gather | solution.py:65
  1771.2 1.5 fusion.30
  1772.8 1.5 convolution_add_fusion.4
  1774.3 1.5 convolution_add_fusion.3
  1775.9 1.6 fusion.26
  1778.6 2.2 exponential_convert_fusion
  1780.8 239.0 %all-reduce.7.cloned.1.call-done = f32[16384]{0:T(1024)} async-done(((f32[16384]{0:T(1024)}), f32[16384]{0:T(1024)}) %all-reduce.7.cloned.1.call-update) | async-done | bytes 65552
  2019.8 0.9 reshape.21
  2020.8 0.6 fusion.54
  2021.4 25.1 %all_gather.35 = bf16[512,64]{1,0:T(8,128)(2,1)S(1)} all-gather(bf16[64,64]{1,0:T(8,128)(2,1)S(1)} %get-tuple-element.16), channel_id=1, replica_groups=mesh['train'=32,'cand'=8] {'cand'}, dimensions={0}, use_global_device_ids=true | all-gather | bytes 73728 | tf_op jit(solution)/shard_map/all_gather | solution.py:87
  2046.5 1.2 fusion.57
  2047.8 2.7 fusion.21
  2050.5 111.4 %reduce-scatter.2.cloned.1.call-done = f32[32,64]{1,0:T(8,128)} async-done(((f32[1024,64]{1,0:T(8,128)}), f32[32,64]{1,0:T(8,128)}) %reduce-scatter.2.cloned.1.call-update) | async-done | bytes 8208 | tf_op jit(solution)/shard_map/reduce_scatter | solution.py:89
  2161.9 1.6 convolution_add_fusion.8
  (37 shorter events, 3.3 us)
Async XLA Ops:
  7.2 27.7 %copy-start = (f32[8,4096]{1,0:T(8,128)S(1)}, f32[8,4096]{1,0:T(8,128)}, u32[]{:S(2)}) copy-start(f32[8,4096]{1,0:T(8,128)} %param.11) | copy-start | bytes 393220
  7.2 82.7 %copy-start.3 = (f32[8,512]{1,0:T(8,128)S(1)}, f32[8,512]{1,0:T(8,128)}, u32[]{:S(2)}) copy-start(f32[8,512]{1,0:T(8,128)} %param.7) | copy-start | bytes 49156
  7.2 741.3 %all-gather.5.cloned.1.call-start = ((), (), s32[]{:S(2)}) async-start(), calls=%async_computation.1 | async-start | bytes 4210688 | tf_op jit(solution)/shard_map/all_gather | solution.py:65
  42.1 955.3 %all-reduce.5.cloned.1.call-start = ((), (), s32[]{:S(2)}) async-start(), calls=%async_computation.4 | async-start | bytes 131072
  92.4 980.9 %copy-start.5 = (f32[8,1024]{1,0:T(8,128)S(1)}, f32[8,1024]{1,0:T(8,128)}, u32[]{:S(2)}) copy-start(f32[8,1024]{1,0:T(8,128)} %param.8) | copy-start | bytes 98308
  755.0 0.6 copy-start.2
  755.7 1015.6 %all-gather.7.cloned.1.call-start = ((), (), s32[]{:S(2)}) async-start(), calls=%async_computation.2 | async-start | bytes 4210688 | tf_op jit(solution)/shard_map/all_gather | solution.py:65
  1073.2 946.6 %all-reduce.7.cloned.1.call-start = ((), (), s32[]{:S(2)}) async-start(), calls=%async_computation.5 | async-start | bytes 131072
  1774.3 273.4 %copy-start.4 = (f32[4096]{0:T(1024)S(1)}, f32[4096]{0:T(1024)}, u32[]{:S(2)}) copy-start(f32[4096]{0:T(1024)} %param.12) | copy-start | bytes 49156
  1777.7 0.6 copy-start.1
  1778.4 383.5 %reduce-scatter.2.cloned.1.call-start = ((), (), s32[]{:S(2)}) async-start(), calls=%async_computation.3 | async-start | bytes 540672 | tf_op jit(solution)/shard_map/reduce_scatter | solution.py:89
Sparse Core Ops, SparseCore 0:
  42.2 706.2 all-gather.4
  755.8 241.5 all-reduce.4
  1073.4 697.8 all-gather.6
  1778.5 241.2 all-reduce.6
  2047.9 113.9 reduce-scatter.1
